TPU v7x, 32 devices: a whole 2x2x4 slice. The times are simulated.
32 devices in a mesh: win: 2 (over y), tile: 4 (over z), sec: 4 (over x, core).
Axes of the slice: x: 2, y: 2, z: 4, core: 2. Of those that a mesh axis runs over, the one named last changes fastest.
Arguments:
- step_field: float32 [64, 2, 32, 256], P(('win', 'sec'), None, 'tile'), parts along dimension 0, may hold values from -4 to 4
- offsets: int32 [64, 2, 2, 32, 256], P(('win', 'sec'), None, None, 'tile'), parts along dimension 0, may hold values from -4 to 4
- fraction: float32 [64, 2, 2, 32, 256], P(('win', 'sec'), None, None, 'tile'), parts along dimension 0, may hold values from 0 to 1
- flow_mask: int32 [64, 2, 32, 256], P(('win', 'sec'), None, 'tile'), parts along dimension 0, may hold values 0 or 1
Outputs:
- displacement: float32 [64, 2, 32, 256], P(('win', 'sec'), None, 'tile'), parts along dimension 0
There are 2 independent parts, one for each index of `win`. A program takes and returns all parts, laid end to end along the dimension named above; each array names one. Nothing has to cross between parts.
All inputs are finite; a program needn't handle non-finite values. No bound on the sum of `flow_mask` on one device may be relied on, other than what follows from the above.
Results may differ from a plain program's by a relative error of at most 0.00002.
Values sent between devices are 32-bit elements; how exact they have to be, the bound alone decides.
A program may use at most 64 MiB of HBM per device.

v0:
```python
import jax
import jax.numpy as jnp
from jax import lax
from jax.sharding import PartitionSpec as P

REACH = 4
ITERS = 4


STEP = 0.25
STIFF_PLANE = 1.0
STIFF_CROSS = 1.0


def carried_in(value, axis, join, neutral):
    count, mine = (lax.axis_size(axis), lax.axis_index(axis))
    pieces = lax.all_gather(value, axis)
    total = jnp.full_like(value, 0) + jnp.asarray(neutral, value.dtype)

    def lap(position, total):
        longer = join(total, pieces[position])
        return jnp.where(position < mine, longer, total)

    return lax.fori_loop(0, count - 1, lap, total)


def with_halo(block, sides, width):
    for axis, dim in sides:
        count = lax.axis_size(axis)
        forward = [(i, i + 1) for i in range(count - 1)]
        backward = [(target, source) for source, target in forward]
        low = lax.ppermute(
            lax.slice_in_dim(block, block.shape[dim] - width, None, axis=dim), axis, forward
        )
        high = lax.ppermute(lax.slice_in_dim(block, 0, width, axis=dim), axis, backward)
        block = jnp.concatenate([low, block, high], axis=dim)
    return block


def interpolate(source, row_off, col_off, row_frac, col_frac, extent):
    margin = extent + 1
    count = row_off.shape[0]
    row_total = row_off.shape[1]
    col_total = row_off.shape[2]
    summed = jnp.zeros((count, 2, row_total, col_total), jnp.float32)
    for shift_row in range(-extent, extent + 2):
        row_weight = jnp.where(row_off == shift_row, 1.0 - row_frac, 0.0) + jnp.where(
            row_off + 1 == shift_row, row_frac, 0.0
        )
        stripe = source[:, :, margin + shift_row : margin + shift_row + row_total, :]
        partial_sum = jnp.zeros((count, 2, row_total, col_total), jnp.float32)
        for shift_col in range(-extent, extent + 2):
            col_weight = jnp.where(col_off == shift_col, 1.0 - col_frac, 0.0) + jnp.where(
                col_off + 1 == shift_col, col_frac, 0.0
            )
            partial_sum = (
                partial_sum
                + col_weight[:, None]
                * stripe[:, :, :, margin + shift_col : margin + shift_col + col_total]
            )
        summed = summed + row_weight[:, None] * partial_sum
    return summed


def node_forces(
    own,
    below,
    above,
    offsets,
    fraction,
    flow_mask,
    first_row,
    first_sec,
    total_rows,
    total_secs,
    extent,
):
    margin = extent + 1
    count = offsets.shape[0]
    row_total = offsets.shape[3]
    col_total = offsets.shape[4]
    center = own[:, :, margin : margin + row_total, margin : margin + col_total]
    global_row = (jnp.arange(row_total, dtype=jnp.int32) + first_row)[:, None]
    column = jnp.arange(col_total, dtype=jnp.int32)[None, :]
    upper = own[:, :, margin - 1 : margin - 1 + row_total, margin : margin + col_total]
    lower = own[:, :, margin + 1 : margin + 1 + row_total, margin : margin + col_total]
    left = own[:, :, margin : margin + row_total, margin - 1 : margin - 1 + col_total]
    right = own[:, :, margin : margin + row_total, margin + 1 : margin + 1 + col_total]
    plane = jnp.where(global_row >= 1, upper - center, 0.0)
    plane = plane + jnp.where(global_row <= total_rows - 2, lower - center, 0.0)
    plane = plane + jnp.where(column >= 1, left - center, 0.0)
    plane = plane + jnp.where(column <= col_total - 2, right - center, 0.0)
    section = jnp.arange(count, dtype=jnp.int32) + first_sec
    cross = jnp.zeros_like(center)
    sources = (below, above)
    for side in range(2):
        row_off = offsets[:, side, 0]
        col_off = offsets[:, side, 1]
        row_frac = fraction[:, side, 0]
        col_frac = fraction[:, side, 1]
        target_row = global_row[None] + row_off
        target_col = column[None] + col_off
        if side == 0:
            section_live = section >= 1
        else:
            section_live = section <= total_secs - 2
        live = (
            (target_row >= 0)
            & (target_row <= total_rows - 2)
            & (target_col >= 0)
            & (target_col <= col_total - 2)
        )
        live = live & (flow_mask[:, side] == 1) & section_live[:, None, None]
        sampled = interpolate(sources[side], row_off, col_off, row_frac, col_frac, extent)
        flow = jnp.stack(
            [row_off.astype(jnp.float32) + row_frac, col_off.astype(jnp.float32) + col_frac], axis=1
        )
        cross = cross + jnp.where(live[:, None], sampled + flow - center, 0.0)
    return STIFF_PLANE * plane + STIFF_CROSS * cross


def add_fields(earlier, later):
    return earlier + later


def per_device(step_field, offsets, fraction, flow_mask):
    sec_count = step_field.shape[0]
    row_count = step_field.shape[2]
    margin = REACH + 1
    running = jnp.cumsum(step_field, axis=0)
    local_total = running[-1]
    prefix = carried_in(local_total, "sec", add_fields, jnp.zeros_like(local_total))
    field = running + prefix[None]
    first_row = lax.axis_index("tile") * row_count
    first_sec = lax.axis_index("sec") * sec_count
    total_rows = row_count * lax.axis_size("tile")
    total_secs = sec_count * lax.axis_size("sec")
    for sweep in range(ITERS):
        rimmed = with_halo(field, (("tile", 2),), margin)
        extended = with_halo(rimmed, (("sec", 0),), 1)
        padded = jnp.pad(extended, ((0, 0), (0, 0), (0, 0), (margin, margin)))
        own = padded[1 : sec_count + 1]
        below = padded[0:sec_count]
        above = padded[2 : sec_count + 2]
        field = field + STEP * node_forces(
            own,
            below,
            above,
            offsets,
            fraction,
            flow_mask,
            first_row,
            first_sec,
            total_rows,
            total_secs,
            REACH,
        )
    return field


def solution(mesh):
    return jax.shard_map(
        per_device,
        mesh=mesh,
        in_specs=(
            P(("win", "sec"), None, "tile", None),
            P(("win", "sec"), None, None, "tile", None),
            P(("win", "sec"), None, None, "tile", None),
            P(("win", "sec"), None, "tile", None),
        ),
        out_specs=P(("win", "sec"), None, "tile", None),
        check_vma=False,
    )
```

profile of v0, /device:TPU:1, one launch (start us, length us, event | category | flops | bytes accessed | tf_op | source)
XLA Modules:
  0.0 110.5 jit_solution(930246442184613591)
XLA Ops:
  0.0 0.9 copy-done
  0.9 1.1 fusion.1045
  2.0 6.0 %all_gather.3 = f32[4,2,8,256]{3,2,1,0:T(8,128)S(1)} all-gather(f32[1,2,8,256]{3,2,1,0:T(8,128)S(1)} %slice.4590), channel_id=1, replica_groups=mesh['win'=2,'tile'=4,'sec'=4] {'sec'}, dimensions={0}, use_global_device_ids=true | all-gather | bytes 81920 | tf_op jit(solution)/shard_map/all_gather | solution.py:17
  8.0 0.1 while.14
  8.2 0.0 copy-start.1
  8.2 0.0 copy-start.2
  8.2 3.9 %collective-permute-start = (f32[8,2,5,256]{3,2,1,0:T(8,128)S(1)}, f32[8,2,5,256]{3,2,1,0:T(8,128)S(1)}, u32[]{:S(2)}, u32[]{:S(2)}) collective-permute-start(f32[8,2,5,256]{3,2,1,0:T(8,128)S(1)} %get-tuple-element.175), channel_id=1, source_target_pairs={{0,4},{4,8},{8,12},{1,5},{5,9},{9,13},{2,6},{6,10},{10,14},{3,7},{... | collective-permute-start | bytes 245768 | tf_op jit(solution)/shard_map/ppermute | solution.py:32
  12.1 1.3 %collective-permute-start.1 = (f32[8,2,5,256]{3,2,1,0:T(8,128)S(1)}, f32[8,2,5,256]{3,2,1,0:T(8,128)S(1)}, u32[]{:S(2)}, u32[]{:S(2)}) collective-permute-start(f32[8,2,5,256]{3,2,1,0:T(8,128)S(1)} %get-tuple-element.176), channel_id=1, source_target_pairs={{4,0},{8,4},{12,8},{5,1},{9,5},{13,9},{6,2},{10,6},{14,10},{7,3},{... | collective-permute-start | bytes 245768 | tf_op jit(solution)/shard_map/ppermute | solution.py:35
  13.5 0.1 fusion.952
  13.6 0.1 fusion.1017
  13.7 0.1 fusion.972
  13.8 0.1 fusion.993
  13.9 0.0 copy-start.3
  13.9 0.1 fusion.1013
  14.0 0.8 copy-done.3
  14.8 0.1 fusion.1035
  15.0 0.0 collective-permute-done
  15.0 3.6 %collective-permute-done.1 = f32[8,2,5,256]{3,2,1,0:T(8,128)S(1)} collective-permute-done((f32[8,2,5,256]{3,2,1,0:T(8,128)S(1)}, f32[8,2,5,256]{3,2,1,0:T(8,128)S(1)}, u32[]{:S(2)}, u32[]{:S(2)}) %collective-permute-start.1) | collective-permute-done | bytes 81952 | tf_op jit(solution)/shard_map/ppermute | solution.py:35
  18.6 4.3 %collective-permute-start.2 = (f32[1,2,18,256]{3,2,1,0:T(8,128)S(1)}, f32[1,2,18,256]{3,2,1,0:T(8,128)S(1)}, u32[]{:S(2)}, u32[]{:S(2)}) collective-permute-start(f32[1,2,18,256]{3,2,1,0:T(8,128)S(1)} %get-tuple-element.167), channel_id=1, source_target_pairs={{0,1},{1,2},{2,3},{4,5},{5,6},{6,7},{8,9},{9,10},{10,11},{12,13},{... | collective-permute-start | bytes 110600 | tf_op jit(solution)/shard_map/ppermute | solution.py:32
  22.9 1.9 %collective-permute-start.3 = (f32[1,2,18,256]{3,2,1,0:T(8,128)S(1)}, f32[1,2,18,256]{3,2,1,0:T(8,128)S(1)}, u32[]{:S(2)}, u32[]{:S(2)}) collective-permute-start(f32[1,2,18,256]{3,2,1,0:T(8,128)S(1)} %get-tuple-element.168), channel_id=1, source_target_pairs={{1,0},{2,1},{3,2},{5,4},{6,5},{7,6},{9,8},{10,9},{11,10},{13,12},{... | collective-permute-start | bytes 110600 | tf_op jit(solution)/shard_map/ppermute | solution.py:35
  24.9 3.5 %collective-permute-done.3 = f32[1,2,18,256]{3,2,1,0:T(8,128)S(1)} collective-permute-done((f32[1,2,18,256]{3,2,1,0:T(8,128)S(1)}, f32[1,2,18,256]{3,2,1,0:T(8,128)S(1)}, u32[]{:S(2)}, u32[]{:S(2)}) %collective-permute-start.3) | collective-permute-done | bytes 36896 | tf_op jit(solution)/shard_map/ppermute | solution.py:35
  28.3 0.4 select_maximum_fusion.12
  28.7 0.1 maximum_maximum_fusion
  28.8 0.7 fusion.921
  29.5 0.1 fusion.943
  30.4 6.0 %fusion.721 = f32[8,2,8,256]{3,2,1,0:T(8,128)S(1)} fusion(f32[8,2,8,256]{3,2,1,0:T(8,128)S(1)} %broadcast_add_fusion, f32[8,2,8,256]{3,2,1,0:T(8,128)S(1)} %broadcast.1290, pred[8,2,8,256]{3,2,1,0:T(8,128)(4,1)S(1)} %broadcast_in_dim.2819, f32[8,2,8,256]{3,2,1,0:T(8,128)S(1)} %broadcast_in_dim.2811, f32[8,2,8,256]{3,2,1,0:T(8,128)S(1)} %get-tuple-element.182, ...), kind=kLoop, calls=%fused_computation.1361 | loop fusion | flops 12779520 | bytes 29851648 | tf_op jit(solution)/shard_map/add | solution.py:145
  36.5 3.2 %collective-permute-start.4 = (f32[8,2,5,256]{3,2,1,0:T(8,128)S(1)}, f32[8,2,5,256]{3,2,1,0:T(8,128)S(1)}, u32[]{:S(2)}, u32[]{:S(2)}) collective-permute-start(f32[8,2,5,256]{3,2,1,0:T(8,128)S(1)} %get-tuple-element.173), channel_id=1, source_target_pairs={{0,4},{4,8},{8,12},{1,5},{5,9},{9,13},{2,6},{6,10},{10,14},{3,7},{... | collective-permute-start | bytes 245768 | tf_op jit(solution)/shard_map/ppermute | solution.py:32
  39.7 1.3 %collective-permute-start.5 = (f32[8,2,5,256]{3,2,1,0:T(8,128)S(1)}, f32[8,2,5,256]{3,2,1,0:T(8,128)S(1)}, u32[]{:S(2)}, u32[]{:S(2)}) collective-permute-start(f32[8,2,5,256]{3,2,1,0:T(8,128)S(1)} %get-tuple-element.174), channel_id=1, source_target_pairs={{4,0},{8,4},{12,8},{5,1},{9,5},{13,9},{6,2},{10,6},{14,10},{7,3},{... | collective-permute-start | bytes 245768 | tf_op jit(solution)/shard_map/ppermute | solution.py:35
  41.0 0.6 collective-permute-done.4
  41.6 3.8 %collective-permute-done.5 = f32[8,2,5,256]{3,2,1,0:T(8,128)S(1)} collective-permute-done((f32[8,2,5,256]{3,2,1,0:T(8,128)S(1)}, f32[8,2,5,256]{3,2,1,0:T(8,128)S(1)}, u32[]{:S(2)}, u32[]{:S(2)}) %collective-permute-start.5) | collective-permute-done | bytes 81952 | tf_op jit(solution)/shard_map/ppermute | solution.py:35
  45.4 3.3 %collective-permute-start.6 = (f32[1,2,18,256]{3,2,1,0:T(8,128)S(1)}, f32[1,2,18,256]{3,2,1,0:T(8,128)S(1)}, u32[]{:S(2)}, u32[]{:S(2)}) collective-permute-start(f32[1,2,18,256]{3,2,1,0:T(8,128)S(1)} %get-tuple-element.163), channel_id=1, source_target_pairs={{0,1},{1,2},{2,3},{4,5},{5,6},{6,7},{8,9},{9,10},{10,11},{12,13},{... | collective-permute-start | bytes 110600 | tf_op jit(solution)/shard_map/ppermute | solution.py:32
  48.7 1.9 %collective-permute-start.7 = (f32[1,2,18,256]{3,2,1,0:T(8,128)S(1)}, f32[1,2,18,256]{3,2,1,0:T(8,128)S(1)}, u32[]{:S(2)}, u32[]{:S(2)}) collective-permute-start(f32[1,2,18,256]{3,2,1,0:T(8,128)S(1)} %get-tuple-element.164), channel_id=1, source_target_pairs={{1,0},{2,1},{3,2},{5,4},{6,5},{7,6},{9,8},{10,9},{11,10},{13,12},{... | collective-permute-start | bytes 110600 | tf_op jit(solution)/shard_map/ppermute | solution.py:35
  50.7 0.0 collective-permute-done.6
  50.7 3.5 %collective-permute-done.7 = f32[1,2,18,256]{3,2,1,0:T(8,128)S(1)} collective-permute-done((f32[1,2,18,256]{3,2,1,0:T(8,128)S(1)}, f32[1,2,18,256]{3,2,1,0:T(8,128)S(1)}, u32[]{:S(2)}, u32[]{:S(2)}) %collective-permute-start.7) | collective-permute-done | bytes 36896 | tf_op jit(solution)/shard_map/ppermute | solution.py:35
  54.1 0.4 select_maximum_fusion.8
  54.5 0.1 maximum_maximum_fusion.1
  54.6 0.7 fusion.684
  55.3 0.1 fusion.706
  55.4 6.0 %fusion.484 = f32[8,2,8,256]{3,2,1,0:T(8,128)S(1)} fusion(f32[8,2,8,256]{3,2,1,0:T(8,128)S(1)} %fusion.721, f32[8,2,8,256]{3,2,1,0:T(8,128)S(1)} %broadcast.1290, pred[8,2,8,256]{3,2,1,0:T(8,128)(4,1)S(1)} %broadcast_in_dim.2819, f32[8,2,8,256]{3,2,1,0:T(8,128)S(1)} %broadcast_in_dim.2811, f32[8,2,8,256]{3,2,1,0:T(8,128)S(1)} %get-tuple-element.182, ...), kind=kLoop, calls=%fused_computation.920 | loop fusion | flops 12779520 | bytes 29851648 | tf_op jit(solution)/shard_map/add | solution.py:145
  61.5 3.2 %collective-permute-start.8 = (f32[8,2,5,256]{3,2,1,0:T(8,128)S(1)}, f32[8,2,5,256]{3,2,1,0:T(8,128)S(1)}, u32[]{:S(2)}, u32[]{:S(2)}) collective-permute-start(f32[8,2,5,256]{3,2,1,0:T(8,128)S(1)} %get-tuple-element.171), channel_id=1, source_target_pairs={{0,4},{4,8},{8,12},{1,5},{5,9},{9,13},{2,6},{6,10},{10,14},{3,7},{... | collective-permute-start | bytes 245768 | tf_op jit(solution)/shard_map/ppermute | solution.py:32
  64.7 1.3 %collective-permute-start.9 = (f32[8,2,5,256]{3,2,1,0:T(8,128)S(1)}, f32[8,2,5,256]{3,2,1,0:T(8,128)S(1)}, u32[]{:S(2)}, u32[]{:S(2)}) collective-permute-start(f32[8,2,5,256]{3,2,1,0:T(8,128)S(1)} %get-tuple-element.172), channel_id=1, source_target_pairs={{4,0},{8,4},{12,8},{5,1},{9,5},{13,9},{6,2},{10,6},{14,10},{7,3},{... | collective-permute-start | bytes 245768 | tf_op jit(solution)/shard_map/ppermute | solution.py:35
  66.0 0.6 collective-permute-done.8
  66.6 3.8 %collective-permute-done.9 = f32[8,2,5,256]{3,2,1,0:T(8,128)S(1)} collective-permute-done((f32[8,2,5,256]{3,2,1,0:T(8,128)S(1)}, f32[8,2,5,256]{3,2,1,0:T(8,128)S(1)}, u32[]{:S(2)}, u32[]{:S(2)}) %collective-permute-start.9) | collective-permute-done | bytes 81952 | tf_op jit(solution)/shard_map/ppermute | solution.py:35
  70.4 3.3 %collective-permute-start.10 = (f32[1,2,18,256]{3,2,1,0:T(8,128)S(1)}, f32[1,2,18,256]{3,2,1,0:T(8,128)S(1)}, u32[]{:S(2)}, u32[]{:S(2)}) collective-permute-start(f32[1,2,18,256]{3,2,1,0:T(8,128)S(1)} %get-tuple-element.159), channel_id=1, source_target_pairs={{0,1},{1,2},{2,3},{4,5},{5,6},{6,7},{8,9},{9,10},{10,11},{12,13},{... | collective-permute-start | bytes 110600 | tf_op jit(solution)/shard_map/ppermute | solution.py:32
  73.7 1.9 %collective-permute-start.11 = (f32[1,2,18,256]{3,2,1,0:T(8,128)S(1)}, f32[1,2,18,256]{3,2,1,0:T(8,128)S(1)}, u32[]{:S(2)}, u32[]{:S(2)}) collective-permute-start(f32[1,2,18,256]{3,2,1,0:T(8,128)S(1)} %get-tuple-element.160), channel_id=1, source_target_pairs={{1,0},{2,1},{3,2},{5,4},{6,5},{7,6},{9,8},{10,9},{11,10},{13,12},{... | collective-permute-start | bytes 110600 | tf_op jit(solution)/shard_map/ppermute | solution.py:35
  75.7 3.5 %collective-permute-done.11 = f32[1,2,18,256]{3,2,1,0:T(8,128)S(1)} collective-permute-done((f32[1,2,18,256]{3,2,1,0:T(8,128)S(1)}, f32[1,2,18,256]{3,2,1,0:T(8,128)S(1)}, u32[]{:S(2)}, u32[]{:S(2)}) %collective-permute-start.11) | collective-permute-done | bytes 36896 | tf_op jit(solution)/shard_map/ppermute | solution.py:35
  79.1 0.4 select_maximum_fusion.4
  79.5 0.1 maximum_maximum_fusion.2
  79.6 0.7 fusion.447
  80.3 0.1 fusion.469
  80.4 6.0 %fusion.247 = f32[8,2,8,256]{3,2,1,0:T(8,128)S(1)} fusion(f32[8,2,8,256]{3,2,1,0:T(8,128)S(1)} %fusion.484, f32[8,2,8,256]{3,2,1,0:T(8,128)S(1)} %broadcast.1290, pred[8,2,8,256]{3,2,1,0:T(8,128)(4,1)S(1)} %broadcast_in_dim.2819, f32[8,2,8,256]{3,2,1,0:T(8,128)S(1)} %broadcast_in_dim.2811, f32[8,2,8,256]{3,2,1,0:T(8,128)S(1)} %get-tuple-element.182, ...), kind=kLoop, calls=%fused_computation.479 | loop fusion | flops 12779520 | bytes 29851648 | tf_op jit(solution)/shard_map/add | solution.py:145
  86.5 1.6 %collective-permute-start.12 = (f32[8,2,5,256]{3,2,1,0:T(8,128)S(1)}, f32[8,2,5,256]{3,2,1,0:T(8,128)S(1)}, u32[]{:S(2)}, u32[]{:S(2)}) collective-permute-start(f32[8,2,5,256]{3,2,1,0:T(8,128)S(1)} %get-tuple-element.169), channel_id=1, source_target_pairs={{0,4},{4,8},{8,12},{1,5},{5,9},{9,13},{2,6},{6,10},{10,14},{3,7},{... | collective-permute-start | bytes 245768 | tf_op jit(solution)/shard_map/ppermute | solution.py:32
  88.1 1.3 %collective-permute-start.13 = (f32[8,2,5,256]{3,2,1,0:T(8,128)S(1)}, f32[8,2,5,256]{3,2,1,0:T(8,128)S(1)}, u32[]{:S(2)}, u32[]{:S(2)}) collective-permute-start(f32[8,2,5,256]{3,2,1,0:T(8,128)S(1)} %get-tuple-element.170), channel_id=1, source_target_pairs={{4,0},{8,4},{12,8},{5,1},{9,5},{13,9},{6,2},{10,6},{14,10},{7,3},{... | collective-permute-start | bytes 245768 | tf_op jit(solution)/shard_map/ppermute | solution.py:35
  89.4 0.6 collective-permute-done.12
  90.0 3.8 %collective-permute-done.13 = f32[8,2,5,256]{3,2,1,0:T(8,128)S(1)} collective-permute-done((f32[8,2,5,256]{3,2,1,0:T(8,128)S(1)}, f32[8,2,5,256]{3,2,1,0:T(8,128)S(1)}, u32[]{:S(2)}, u32[]{:S(2)}) %collective-permute-start.13) | collective-permute-done | bytes 81952 | tf_op jit(solution)/shard_map/ppermute | solution.py:35
  93.8 3.3 %collective-permute-start.14 = (f32[1,2,18,256]{3,2,1,0:T(8,128)S(1)}, f32[1,2,18,256]{3,2,1,0:T(8,128)S(1)}, u32[]{:S(2)}, u32[]{:S(2)}) collective-permute-start(f32[1,2,18,256]{3,2,1,0:T(8,128)S(1)} %get-tuple-element.155), channel_id=1, source_target_pairs={{0,1},{1,2},{2,3},{4,5},{5,6},{6,7},{8,9},{9,10},{10,11},{12,13},{... | collective-permute-start | bytes 110600 | tf_op jit(solution)/shard_map/ppermute | solution.py:32
  97.2 2.1 %collective-permute-start.15 = (f32[1,2,18,256]{3,2,1,0:T(8,128)S(1)}, f32[1,2,18,256]{3,2,1,0:T(8,128)S(1)}, u32[]{:S(2)}, u32[]{:S(2)}) collective-permute-start(f32[1,2,18,256]{3,2,1,0:T(8,128)S(1)} %get-tuple-element.156), channel_id=1, source_target_pairs={{1,0},{2,1},{3,2},{5,4},{6,5},{7,6},{9,8},{10,9},{11,10},{13,12},{... | collective-permute-start | bytes 110600 | tf_op jit(solution)/shard_map/ppermute | solution.py:35
  99.3 0.0 collective-permute-done.14
  99.3 3.3 %collective-permute-done.15 = f32[1,2,18,256]{3,2,1,0:T(8,128)S(1)} collective-permute-done((f32[1,2,18,256]{3,2,1,0:T(8,128)S(1)}, f32[1,2,18,256]{3,2,1,0:T(8,128)S(1)}, u32[]{:S(2)}, u32[]{:S(2)}) %collective-permute-start.15) | collective-permute-done | bytes 36896 | tf_op jit(solution)/shard_map/ppermute | solution.py:35
  102.6 0.4 select_maximum_fusion
  102.9 0.1 maximum_maximum_fusion.3
  103.0 0.7 fusion.210
  103.7 0.1 fusion.232
  103.9 6.6 %fusion.10 = f32[8,2,8,256]{3,2,1,0:T(8,128)} fusion(f32[8,2,8,256]{3,2,1,0:T(8,128)S(1)} %fusion.247, f32[8,2,8,256]{3,2,1,0:T(8,128)S(1)} %broadcast.1290, pred[8,2,8,256]{3,2,1,0:T(8,128)(4,1)S(1)} %broadcast_in_dim.2819, f32[8,2,8,256]{3,2,1,0:T(8,128)S(1)} %broadcast_in_dim.2811, f32[8,2,8,256]{3,2,1,0:T(8,128)S(1)} %get-tuple-element.182, ...), kind=kLoop, calls=%fused_computation.38 | loop fusion | flops 12779520 | bytes 29851648 | tf_op jit(solution)/shard_map/add | solution.py:145
  (70 shorter events, 0.8 us)
Async XLA Ops:
  0.0 0.9 copy-start
  8.2 5.3 %copy-start.1 = (s32[8,2,2,8,256]{4,3,2,1,0:T(8,128)S(1)}, s32[8,2,2,8,256]{4,3,2,1,0:T(8,128)}, u32[]{:S(2)}) copy-start(s32[8,2,2,8,256]{4,3,2,1,0:T(8,128)} %param.7) | copy-start | bytes 786436
  8.2 5.3 %copy-start.2 = (f32[8,2,2,8,256]{4,3,2,1,0:T(8,128)S(1)}, f32[8,2,2,8,256]{4,3,2,1,0:T(8,128)}, u32[]{:S(2)}) copy-start(f32[8,2,2,8,256]{4,3,2,1,0:T(8,128)} %param.8) | copy-start | bytes 786436
  8.2 6.8 %collective-permute-start = (f32[8,2,5,256]{3,2,1,0:T(8,128)S(1)}, f32[8,2,5,256]{3,2,1,0:T(8,128)S(1)}, u32[]{:S(2)}, u32[]{:S(2)}) collective-permute-start(f32[8,2,5,256]{3,2,1,0:T(8,128)S(1)} %get-tuple-element.175), channel_id=1, source_target_pairs={{0,4},{4,8},{8,12},{1,5},{5,9},{9,13},{2,6},{6,10},{10,14},{3,7},{... | collective-permute-start | bytes 245768 | tf_op jit(solution)/shard_map/ppermute | solution.py:32
  12.1 6.5 %collective-permute-start.1 = (f32[8,2,5,256]{3,2,1,0:T(8,128)S(1)}, f32[8,2,5,256]{3,2,1,0:T(8,128)S(1)}, u32[]{:S(2)}, u32[]{:S(2)}) collective-permute-start(f32[8,2,5,256]{3,2,1,0:T(8,128)S(1)} %get-tuple-element.176), channel_id=1, source_target_pairs={{4,0},{8,4},{12,8},{5,1},{9,5},{13,9},{6,2},{10,6},{14,10},{7,3},{... | collective-permute-start | bytes 245768 | tf_op jit(solution)/shard_map/ppermute | solution.py:35
  13.9 0.9 copy-start.3
  18.6 6.2 %collective-permute-start.2 = (f32[1,2,18,256]{3,2,1,0:T(8,128)S(1)}, f32[1,2,18,256]{3,2,1,0:T(8,128)S(1)}, u32[]{:S(2)}, u32[]{:S(2)}) collective-permute-start(f32[1,2,18,256]{3,2,1,0:T(8,128)S(1)} %get-tuple-element.167), channel_id=1, source_target_pairs={{0,1},{1,2},{2,3},{4,5},{5,6},{6,7},{8,9},{9,10},{10,11},{12,13},{... | collective-permute-start | bytes 110600 | tf_op jit(solution)/shard_map/ppermute | solution.py:32
  22.9 5.4 %collective-permute-start.3 = (f32[1,2,18,256]{3,2,1,0:T(8,128)S(1)}, f32[1,2,18,256]{3,2,1,0:T(8,128)S(1)}, u32[]{:S(2)}, u32[]{:S(2)}) collective-permute-start(f32[1,2,18,256]{3,2,1,0:T(8,128)S(1)} %get-tuple-element.168), channel_id=1, source_target_pairs={{1,0},{2,1},{3,2},{5,4},{6,5},{7,6},{9,8},{10,9},{11,10},{13,12},{... | collective-permute-start | bytes 110600 | tf_op jit(solution)/shard_map/ppermute | solution.py:35
  36.5 5.1 %collective-permute-start.4 = (f32[8,2,5,256]{3,2,1,0:T(8,128)S(1)}, f32[8,2,5,256]{3,2,1,0:T(8,128)S(1)}, u32[]{:S(2)}, u32[]{:S(2)}) collective-permute-start(f32[8,2,5,256]{3,2,1,0:T(8,128)S(1)} %get-tuple-element.173), channel_id=1, source_target_pairs={{0,4},{4,8},{8,12},{1,5},{5,9},{9,13},{2,6},{6,10},{10,14},{3,7},{... | collective-permute-start | bytes 245768 | tf_op jit(solution)/shard_map/ppermute | solution.py:32
  39.7 5.7 %collective-permute-start.5 = (f32[8,2,5,256]{3,2,1,0:T(8,128)S(1)}, f32[8,2,5,256]{3,2,1,0:T(8,128)S(1)}, u32[]{:S(2)}, u32[]{:S(2)}) collective-permute-start(f32[8,2,5,256]{3,2,1,0:T(8,128)S(1)} %get-tuple-element.174), channel_id=1, source_target_pairs={{4,0},{8,4},{12,8},{5,1},{9,5},{13,9},{6,2},{10,6},{14,10},{7,3},{... | collective-permute-start | bytes 245768 | tf_op jit(solution)/shard_map/ppermute | solution.py:35
  45.4 5.3 %collective-permute-start.6 = (f32[1,2,18,256]{3,2,1,0:T(8,128)S(1)}, f32[1,2,18,256]{3,2,1,0:T(8,128)S(1)}, u32[]{:S(2)}, u32[]{:S(2)}) collective-permute-start(f32[1,2,18,256]{3,2,1,0:T(8,128)S(1)} %get-tuple-element.163), channel_id=1, source_target_pairs={{0,1},{1,2},{2,3},{4,5},{5,6},{6,7},{8,9},{9,10},{10,11},{12,13},{... | collective-permute-start | bytes 110600 | tf_op jit(solution)/shard_map/ppermute | solution.py:32
  48.7 5.4 %collective-permute-start.7 = (f32[1,2,18,256]{3,2,1,0:T(8,128)S(1)}, f32[1,2,18,256]{3,2,1,0:T(8,128)S(1)}, u32[]{:S(2)}, u32[]{:S(2)}) collective-permute-start(f32[1,2,18,256]{3,2,1,0:T(8,128)S(1)} %get-tuple-element.164), channel_id=1, source_target_pairs={{1,0},{2,1},{3,2},{5,4},{6,5},{7,6},{9,8},{10,9},{11,10},{13,12},{... | collective-permute-start | bytes 110600 | tf_op jit(solution)/shard_map/ppermute | solution.py:35
  61.5 5.1 %collective-permute-start.8 = (f32[8,2,5,256]{3,2,1,0:T(8,128)S(1)}, f32[8,2,5,256]{3,2,1,0:T(8,128)S(1)}, u32[]{:S(2)}, u32[]{:S(2)}) collective-permute-start(f32[8,2,5,256]{3,2,1,0:T(8,128)S(1)} %get-tuple-element.171), channel_id=1, source_target_pairs={{0,4},{4,8},{8,12},{1,5},{5,9},{9,13},{2,6},{6,10},{10,14},{3,7},{... | collective-permute-start | bytes 245768 | tf_op jit(solution)/shard_map/ppermute | solution.py:32
  64.7 5.7 %collective-permute-start.9 = (f32[8,2,5,256]{3,2,1,0:T(8,128)S(1)}, f32[8,2,5,256]{3,2,1,0:T(8,128)S(1)}, u32[]{:S(2)}, u32[]{:S(2)}) collective-permute-start(f32[8,2,5,256]{3,2,1,0:T(8,128)S(1)} %get-tuple-element.172), channel_id=1, source_target_pairs={{4,0},{8,4},{12,8},{5,1},{9,5},{13,9},{6,2},{10,6},{14,10},{7,3},{... | collective-permute-start | bytes 245768 | tf_op jit(solution)/shard_map/ppermute | solution.py:35
  70.4 5.3 %collective-permute-start.10 = (f32[1,2,18,256]{3,2,1,0:T(8,128)S(1)}, f32[1,2,18,256]{3,2,1,0:T(8,128)S(1)}, u32[]{:S(2)}, u32[]{:S(2)}) collective-permute-start(f32[1,2,18,256]{3,2,1,0:T(8,128)S(1)} %get-tuple-element.159), channel_id=1, source_target_pairs={{0,1},{1,2},{2,3},{4,5},{5,6},{6,7},{8,9},{9,10},{10,11},{12,13},{... | collective-permute-start | bytes 110600 | tf_op jit(solution)/shard_map/ppermute | solution.py:32
  73.7 5.4 %collective-permute-start.11 = (f32[1,2,18,256]{3,2,1,0:T(8,128)S(1)}, f32[1,2,18,256]{3,2,1,0:T(8,128)S(1)}, u32[]{:S(2)}, u32[]{:S(2)}) collective-permute-start(f32[1,2,18,256]{3,2,1,0:T(8,128)S(1)} %get-tuple-element.160), channel_id=1, source_target_pairs={{1,0},{2,1},{3,2},{5,4},{6,5},{7,6},{9,8},{10,9},{11,10},{13,12},{... | collective-permute-start | bytes 110600 | tf_op jit(solution)/shard_map/ppermute | solution.py:35
  86.5 3.6 %collective-permute-start.12 = (f32[8,2,5,256]{3,2,1,0:T(8,128)S(1)}, f32[8,2,5,256]{3,2,1,0:T(8,128)S(1)}, u32[]{:S(2)}, u32[]{:S(2)}) collective-permute-start(f32[8,2,5,256]{3,2,1,0:T(8,128)S(1)} %get-tuple-element.169), channel_id=1, source_target_pairs={{0,4},{4,8},{8,12},{1,5},{5,9},{9,13},{2,6},{6,10},{10,14},{3,7},{... | collective-permute-start | bytes 245768 | tf_op jit(solution)/shard_map/ppermute | solution.py:32
  88.1 5.7 %collective-permute-start.13 = (f32[8,2,5,256]{3,2,1,0:T(8,128)S(1)}, f32[8,2,5,256]{3,2,1,0:T(8,128)S(1)}, u32[]{:S(2)}, u32[]{:S(2)}) collective-permute-start(f32[8,2,5,256]{3,2,1,0:T(8,128)S(1)} %get-tuple-element.170), channel_id=1, source_target_pairs={{4,0},{8,4},{12,8},{5,1},{9,5},{13,9},{6,2},{10,6},{14,10},{7,3},{... | collective-permute-start | bytes 245768 | tf_op jit(solution)/shard_map/ppermute | solution.py:35
  93.8 5.4 %collective-permute-start.14 = (f32[1,2,18,256]{3,2,1,0:T(8,128)S(1)}, f32[1,2,18,256]{3,2,1,0:T(8,128)S(1)}, u32[]{:S(2)}, u32[]{:S(2)}) collective-permute-start(f32[1,2,18,256]{3,2,1,0:T(8,128)S(1)} %get-tuple-element.155), channel_id=1, source_target_pairs={{0,1},{1,2},{2,3},{4,5},{5,6},{6,7},{8,9},{9,10},{10,11},{12,13},{... | collective-permute-start | bytes 110600 | tf_op jit(solution)/shard_map/ppermute | solution.py:32
  97.2 5.4 %collective-permute-start.15 = (f32[1,2,18,256]{3,2,1,0:T(8,128)S(1)}, f32[1,2,18,256]{3,2,1,0:T(8,128)S(1)}, u32[]{:S(2)}, u32[]{:S(2)}) collective-permute-start(f32[1,2,18,256]{3,2,1,0:T(8,128)S(1)} %get-tuple-element.156), channel_id=1, source_target_pairs={{1,0},{2,1},{3,2},{5,4},{6,5},{7,6},{9,8},{10,9},{11,10},{13,12},{... | collective-permute-start | bytes 110600 | tf_op jit(solution)/shard_map/ppermute | solution.py:35
where the time goes:
time: 111 us; the launch traced here: 110 us
  starting transfers between devices  39.2 us (35%)
  other arithmetic  31.5 us (28%)
  waiting for transfers between devices  30.6 us (28%)
  blocking collectives  6.04 us (5%)
  local copies, waits for them, and re-layouts  2.22 us (2%)
    ppermute x8, waiting for transfers between devices, with_halo(): lax.ppermute(lax.slice_in_dim(block, 0, width, axis=dim), axis, backward)  28.7 us
    ppermute x8, starting transfers between devices, with_halo(): lax.ppermute(lax.slice_in_dim(block, block.shape[dim] - width, None, axis...  26.2 us
    add x4, other arithmetic, per_device(): field + STEP * node_forces(own, below, above, offsets, fraction, flow_mas...  24.6 us
    ppermute x8, starting transfers between devices, with_halo(): lax.ppermute(lax.slice_in_dim(block, 0, width, axis=dim), axis, backward)  13 us
    all_gather x1, blocking collectives, carried_in(): pieces = lax.all_gather(value, axis)  6.04 us
    add x4, other arithmetic, interpolate(): summed = summed + row_weight[:, None] * partial_sum  2.72 us
  transfers between devices with their start and end apart: 16, of which 11 were waited for; matrix products, arithmetic and copies ran while one was open for 1% of the time, Pallas kernels for 0%

commit v1 on v0

v1 whole, which is shorter than its diff:
```python
import functools

import jax
import jax.numpy as jnp
from jax import lax
from jax.experimental import pallas as pl
from jax.experimental.pallas import tpu as pltpu
from jax.sharding import PartitionSpec as P

REACH = 4
ITERS = 4
STEP = 0.25
ROWS = 8
LANES = 128
SHIFTS = 2 * REACH + 2
MESH = pl.DeviceIdType.MESH
DIRECTIONS = ((0, 1), (0, -1), (1, 1), (1, -1), (-1, 1), (-1, -1), (1, 0), (-1, 0))


def lane_ids():
    return lax.broadcasted_iota(jnp.int32, (ROWS, LANES), 1)


def middle_of(a0, b0, a1, b1):
    lane = lax.broadcasted_iota(jnp.int32, a0.shape, 1)
    first = pltpu.roll(jnp.where(lane >= 64, a0, b0), 32, 1)
    second = pltpu.roll(jnp.where(lane >= 64, a1, b1), 96, 1)
    return jnp.where(lane < 64, first, second)


def pick(values, index):
    return jnp.take_along_axis(values, index, axis=1, mode="promise_in_bounds")


def kernel(
    n_tile, n_sec, step_ref, off_ref, frac_ref, mask_ref, out_ref,
    field, totals, base, index0, index1, col_frac, row_weight, flow_sum, degree,
    send_sem, recv_sem, total_send, total_recv,
):
    count = step_ref.shape[0]
    tile = lax.axis_index("tile")
    sec = lax.axis_index("sec")

    def there(dt, ds):
        ok = None
        for here, d, n in ((tile, dt, n_tile), (sec, ds, n_sec)):
            if d:
                test = here + d < n if d > 0 else here + d >= 0
                ok = test if ok is None else jnp.logical_and(ok, test)
        return ok

    @pl.when(tile == 0)
    def _():
        field[:, :, :, 0:ROWS, :] = jnp.zeros((ITERS, count + 2, 5, ROWS, LANES), jnp.float32)

    @pl.when(tile == n_tile - 1)
    def _():
        field[:, :, :, 2 * ROWS:, :] = jnp.zeros((ITERS, count + 2, 5, ROWS, LANES), jnp.float32)

    @pl.when(sec == 0)
    def _():
        field[:, 0] = jnp.zeros((ITERS, 5, 3 * ROWS, LANES), jnp.float32)

    @pl.when(sec == n_sec - 1)
    def _():
        field[:, count + 1] = jnp.zeros((ITERS, 5, 3 * ROWS, LANES), jnp.float32)

    barrier = pltpu.get_barrier_semaphore()

    def greet(peer):
        pl.semaphore_signal(barrier, inc=1, device_id=peer, device_id_type=MESH)

    for dt, ds in DIRECTIONS:
        if dt:

            @pl.when(there(dt, ds))
            def _():
                greet({"tile": tile + dt, "sec": sec + ds})

    for other in range(n_sec):

        @pl.when(sec != other)
        def _():
            greet({"sec": other})

    def beside(here, n):
        return jnp.where(here > 0, 1, 0) + jnp.where(here < n - 1, 1, 0)

    pl.semaphore_wait(barrier, n_sec - 1 + beside(tile, n_tile) * (1 + beside(sec, n_sec)))

    for c in range(2):
        for h in range(2):
            k = 2 * c + h
            running = step_ref[0, c, :, h * LANES:(h + 1) * LANES]
            field[0, 1, k, ROWS:2 * ROWS, :] = running
            for s in range(1, count):
                running = running + step_ref[s, c, :, h * LANES:(h + 1) * LANES]
                field[0, s + 1, k, ROWS:2 * ROWS, :] = running
            base[k] = running

    def total_copy(source, target):
        return pltpu.make_async_remote_copy(
            src_ref=base, dst_ref=totals.at[source], send_sem=total_send.at[target],
            recv_sem=total_recv.at[source], device_id={"sec": target}, device_id_type=MESH,
        )

    for source in range(n_sec - 1):

        @pl.when(sec == source)
        def _():
            for target in range(source + 1, n_sec):
                total_copy(source, target).start()

    lane = lane_ids()
    row = lax.broadcasted_iota(jnp.int32, (ROWS, LANES), 0) + tile * ROWS
    last_row = n_tile * ROWS - 1
    last_col = 2 * LANES - 1

    def prepare(s, carry):
        flows = [[jnp.zeros((ROWS, LANES), jnp.float32) for _ in range(2)] for _ in range(2)]
        live_count = []
        for h in range(2):
            column = lane + h * LANES
            four = jnp.where(row >= 1, 1.0, 0.0) + jnp.where(row <= last_row - 1, 1.0, 0.0)
            four = four + jnp.where(column >= 1, 1.0, 0.0) + jnp.where(column <= last_col - 1, 1.0, 0.0)
            live_count.append(four)
        for side in range(2):
            j = 2 * s + side
            if side == 0:
                section_live = jnp.logical_or(sec > 0, s >= 1)
            else:
                section_live = jnp.logical_or(sec < n_sec - 1, s <= count - 2)
            halves = []
            for h in range(2):
                part = slice(h * LANES, (h + 1) * LANES)
                ro, co = off_ref[s, side, 0, :, part], off_ref[s, side, 1, :, part]
                rf, cf = frac_ref[s, side, 0, :, part], frac_ref[s, side, 1, :, part]
                target_row, target_col = row + ro, lane + h * LANES + co
                live = (target_row >= 0) & (target_row <= last_row - 1)
                live = live & (target_col >= 0) & (target_col <= last_col - 1)
                live = live & (mask_ref[s, side, :, part] == 1)
                gain = jnp.where(section_live, 1.0, 0.0)
                live = jnp.where(live, 1.0, 0.0) * gain
                flows[0][h] = flows[0][h] + live * (ro.astype(jnp.float32) + rf)
                flows[1][h] = flows[1][h] + live * (co.astype(jnp.float32) + cf)
                live_count[h] = live_count[h] + live
                halves.append((ro, co, live * (1.0 - rf), live * rf, cf))
            a, b = halves
            halves.append(tuple(middle_of(x, y, x, y) for x, y in zip(a, b)))
            for t, (ro, co, low, high, cf) in enumerate(halves):
                index0[j, t] = jnp.clip(lane + co, 0, LANES - 1)
                index1[j, t] = jnp.clip(lane + co + 1, 0, LANES - 1)
                col_frac[j, t] = cf
                for d in range(SHIFTS):
                    shift = d - REACH
                    row_weight[j, t, d] = jnp.where(ro == shift, low, jnp.where(ro == shift - 1, high, 0.0))
        for h in range(2):
            degree[s, h] = live_count[h]
            for c in range(2):
                flow_sum[s, 2 * c + h] = flows[c][h]
        return carry

    lax.fori_loop(0, count, prepare, 0)

    for source in range(n_sec - 1):

        @pl.when(sec > source)
        def _():
            total_copy(source, source + 1).wait_recv()

        @pl.when(sec == source)
        def _():
            for target in range(source + 1, n_sec):
                total_copy(source, target).wait_send()

    base[...] = jnp.zeros(base.shape, jnp.float32)
    for source in range(n_sec - 1):

        @pl.when(sec > source)
        def _():
            base[...] = base[...] + totals[source]

    for s in range(count):
        for k in range(4):
            field[0, s + 1, k, ROWS:2 * ROWS, :] = field[0, s + 1, k, ROWS:2 * ROWS, :] + base[k]

    def halo_copy(sweep, number):
        dt, ds = DIRECTIONS[number]
        if ds == 0:
            source = target = pl.ds(1, count)
        elif ds > 0:
            source, target = pl.ds(count, 1), pl.ds(0, 1)
        else:
            source, target = pl.ds(1, 1), pl.ds(count + 1, 1)
        landing = pl.ds({1: 0, 0: ROWS, -1: 2 * ROWS}[dt], ROWS)
        peer = {}
        if dt:
            peer["tile"] = tile + dt
        if ds:
            peer["sec"] = sec + ds
        return pltpu.make_async_remote_copy(
            src_ref=field.at[sweep, source, pl.ds(0, 4), pl.ds(ROWS, ROWS)],
            dst_ref=field.at[sweep, target, pl.ds(0, 4), landing],
            send_sem=send_sem.at[sweep, number], recv_sem=recv_sem.at[sweep, number],
            device_id=peer, device_id_type=MESH,
        )

    for sweep in range(ITERS):
        for number, (dt, ds) in enumerate(DIRECTIONS):

            @pl.when(there(dt, ds))
            def _():
                halo_copy(sweep, number).start()

        for number, (dt, ds) in enumerate(DIRECTIONS):

            @pl.when(there(-dt, -ds))
            def _():
                halo_copy(sweep, number).wait_recv()

        def middle(slot, carry):
            parts = [field[sweep, slot, k] for k in range(4)]
            field[sweep, slot, 4] = middle_of(*parts)
            return carry

        lax.fori_loop(0, count + 2, middle, 0)

        def relax(s, carry):
            sums = [None] * 5
            for side in range(2):
                j = 2 * s + side
                slot = s + 2 * side
                i0 = [index0[j, t] for t in range(3)]
                i1 = [index1[j, t] for t in range(3)]
                cf = [col_frac[j, t] for t in range(3)]
                for d in range(SHIFTS):
                    top = ROWS - REACH + d
                    weight = [row_weight[j, t, d] for t in range(3)]
                    for k in range(5):
                        t = 2 if k == 4 else k % 2
                        source = field[sweep, slot, k, top:top + ROWS, :]
                        low, high = pick(source, i0[t]), pick(source, i1[t])
                        term = weight[t] * (low + cf[t] * (high - low))
                        sums[k] = term if sums[k] is None else sums[k] + term
            for c in range(2):
                seam = pltpu.roll(sums[4], 96 if c == 0 else 32, 1)
                cross = (
                    jnp.where(lane < 112, sums[2 * c], seam),
                    jnp.where(lane < 16, seam, sums[2 * c + 1]),
                )
                own = [field[sweep, s + 1, 2 * c + h, ROWS:2 * ROWS, :] for h in range(2)]
                left = [pltpu.roll(x, 1, 1) for x in own]
                right = [pltpu.roll(x, LANES - 1, 1) for x in own]
                sides = (
                    jnp.where(lane == 0, 0.0, left[0]) + jnp.where(lane == LANES - 1, right[1], right[0]),
                    jnp.where(lane == 0, left[0], left[1]) + jnp.where(lane == LANES - 1, 0.0, right[1]),
                )
                for h in range(2):
                    k = 2 * c + h
                    above = field[sweep, s + 1, k, ROWS - 1:2 * ROWS - 1, :]
                    below = field[sweep, s + 1, k, ROWS + 1:2 * ROWS + 1, :]
                    force = cross[h] + flow_sum[s, k] + sides[h] + (above + below) - degree[s, h] * own[h]
                    new = own[h] + STEP * force
                    if sweep == ITERS - 1:
                        out_ref[s, c, :, h * LANES:(h + 1) * LANES] = new
                    else:
                        field[sweep + 1, s + 1, k, ROWS:2 * ROWS, :] = new
            return carry

        lax.fori_loop(0, count, relax, 0)

    for sweep in range(ITERS):
        for number, (dt, ds) in enumerate(DIRECTIONS):

            @pl.when(there(dt, ds))
            def _():
                halo_copy(sweep, number).wait_send()


def per_device(n_tile, n_sec, step_field, offsets, fraction, flow_mask):
    count = step_field.shape[0]
    vmem = pl.BlockSpec(memory_space=pltpu.VMEM)
    f32, i32 = jnp.float32, jnp.int32
    return pl.pallas_call(
        functools.partial(kernel, n_tile, n_sec),
        out_shape=jax.ShapeDtypeStruct(step_field.shape, f32),
        in_specs=[vmem] * 4,
        out_specs=vmem,
        scratch_shapes=[
            pltpu.VMEM((ITERS, count + 2, 5, 3 * ROWS, LANES), f32),
            pltpu.VMEM((n_sec, 4, ROWS, LANES), f32),
            pltpu.VMEM((4, ROWS, LANES), f32),
            pltpu.VMEM((2 * count, 3, ROWS, LANES), i32),
            pltpu.VMEM((2 * count, 3, ROWS, LANES), i32),
            pltpu.VMEM((2 * count, 3, ROWS, LANES), f32),
            pltpu.VMEM((2 * count, 3, SHIFTS, ROWS, LANES), f32),
            pltpu.VMEM((count, 4, ROWS, LANES), f32),
            pltpu.VMEM((count, 2, ROWS, LANES), f32),
            pltpu.SemaphoreType.DMA((ITERS, len(DIRECTIONS))),
            pltpu.SemaphoreType.DMA((ITERS, len(DIRECTIONS))),
            pltpu.SemaphoreType.DMA((n_sec,)),
            pltpu.SemaphoreType.DMA((n_sec,)),
        ],
        compiler_params=pltpu.CompilerParams(
            collective_id=0, has_side_effects=True, vmem_limit_bytes=32 * 1024 * 1024
        ),
    )(step_field, offsets, fraction, flow_mask)


def solution(mesh):
    spec = P(("win", "sec"), None, "tile", None)
    flow_spec = P(("win", "sec"), None, None, "tile", None)
    return jax.shard_map(
        functools.partial(per_device, mesh.shape["tile"], mesh.shape["sec"]),
        mesh=mesh,
        in_specs=(spec, flow_spec, flow_spec, spec),
        out_specs=spec,
        check_vma=False,
    )
```

time: 111 us -> 55.2 us (0.50)
  the two profiles are of different devices: /device:TPU:1 before, /device:TPU:0 now
where the time goes in v1:
time: 55.2 us; the launch traced here: 55 us
  Pallas kernels  50.6 us (92%)
  local copies, waits for them, and re-layouts  4.36 us (8%)
    pallas_call x1, Pallas kernels, per_device(): pl.pallas_call(functools.partial(kernel, n_tile, n_sec), out_shape=jax.Sh...  50.6 us
    unnamed x9, local copies, waits for them, and re-layouts  4.36 us

profile of v1, /device:TPU:0, one launch (start us, length us, event | category | flops | bytes accessed | tf_op | source)
XLA Modules:
  0.0 55.0 jit_solution(9980121077052299586)
XLA Ops:
  0.0 0.0 copy-start
  0.0 0.9 %copy-done = s32[8,2,2,8,256]{4,3,2,1,0:T(8,128)S(1)} copy-done((s32[8,2,2,8,256]{4,3,2,1,0:T(8,128)S(1)}, s32[8,2,2,8,256]{4,3,2,1,0:T(8,128)}, u32[]{:S(2)}) %copy-start) | copy-done | bytes 262168
  1.0 0.0 copy-start.1
  1.0 0.9 %copy-done.1 = f32[8,2,2,8,256]{4,3,2,1,0:T(8,128)S(1)} copy-done((f32[8,2,2,8,256]{4,3,2,1,0:T(8,128)S(1)}, f32[8,2,2,8,256]{4,3,2,1,0:T(8,128)}, u32[]{:S(2)}) %copy-start.1) | copy-done | bytes 262168
  1.9 0.0 copy-start.2
  1.9 0.9 %copy-done.2 = f32[8,2,8,256]{3,2,1,0:T(8,128)S(1)} copy-done((f32[8,2,8,256]{3,2,1,0:T(8,128)S(1)}, f32[8,2,8,256]{3,2,1,0:T(8,128)}, u32[]{:S(2)}) %copy-start.2) | copy-done | bytes 131096
  2.8 0.0 copy-start.3
  2.8 0.9 %copy-done.3 = s32[8,2,8,256]{3,2,1,0:T(8,128)S(1)} copy-done((s32[8,2,8,256]{3,2,1,0:T(8,128)S(1)}, s32[8,2,8,256]{3,2,1,0:T(8,128)}, u32[]{:S(2)}) %copy-start.3) | copy-done | bytes 131096
  3.7 50.6 %shard_map.46 = f32[8,2,8,256]{3,2,1,0:T(8,128)S(1)} custom-call(f32[8,2,8,256]{3,2,1,0:T(8,128)S(1)} %copy-done.2, s32[8,2,2,8,256]{4,3,2,1,0:T(8,128)S(1)} %copy-done, f32[8,2,2,8,256]{4,3,2,1,0:T(8,128)S(1)} %copy-done.1, s32[8,2,8,256]{3,2,1,0:T(8,128)S(1)} %copy-done.3), custom_call_target="tpu_custom_call" | custom-call | tf_op jit(solution)/shard_map/pallas_call | solution.py:284
  54.3 0.7 %copy.6 = f32[8,2,8,256]{3,2,1,0:T(8,128)} copy(f32[8,2,8,256]{3,2,1,0:T(8,128)S(1)} %shard_map.46) | data formatting | bytes 262144
Async XLA Ops:
  0.0 0.9 %copy-start = (s32[8,2,2,8,256]{4,3,2,1,0:T(8,128)S(1)}, s32[8,2,2,8,256]{4,3,2,1,0:T(8,128)}, u32[]{:S(2)}) copy-start(s32[8,2,2,8,256]{4,3,2,1,0:T(8,128)} %off_ref.1) | copy-start | bytes 786436
  1.0 0.9 %copy-start.1 = (f32[8,2,2,8,256]{4,3,2,1,0:T(8,128)S(1)}, f32[8,2,2,8,256]{4,3,2,1,0:T(8,128)}, u32[]{:S(2)}) copy-start(f32[8,2,2,8,256]{4,3,2,1,0:T(8,128)} %frac_ref.1) | copy-start | bytes 786436
  1.9 0.9 %copy-start.2 = (f32[8,2,8,256]{3,2,1,0:T(8,128)S(1)}, f32[8,2,8,256]{3,2,1,0:T(8,128)}, u32[]{:S(2)}) copy-start(f32[8,2,8,256]{3,2,1,0:T(8,128)} %step_ref.1) | copy-start | bytes 393220
  2.8 0.9 %copy-start.3 = (s32[8,2,8,256]{3,2,1,0:T(8,128)S(1)}, s32[8,2,8,256]{3,2,1,0:T(8,128)}, u32[]{:S(2)}) copy-start(s32[8,2,8,256]{3,2,1,0:T(8,128)} %mask_ref.1) | copy-start | bytes 393220

commit v2 on v1

v2 whole, which is shorter than its diff:
```python
import functools

import jax
import jax.numpy as jnp
from jax import lax
from jax.experimental import pallas as pl
from jax.experimental.pallas import tpu as pltpu
from jax.sharding import PartitionSpec as P

REACH = 4
ITERS = 4
STEP = 0.25
ROWS = 8
UP = REACH
DOWN = REACH + 1
LANES = 128
SHIFTS = 2 * REACH + 2
MESH = pl.DeviceIdType.MESH
DIRECTIONS = ((0, 1), (0, -1), (1, 1), (1, -1), (-1, 1), (-1, -1), (1, 0), (-1, 0))


def middle_of(a0, b0, a1, b1):
    lane = lax.broadcasted_iota(jnp.int32, a0.shape, 1)
    first = pltpu.roll(jnp.where(lane >= 64, a0, b0), 32, 1)
    second = pltpu.roll(jnp.where(lane >= 64, a1, b1), 96, 1)
    return jnp.where(lane < 64, first, second)


def pick(values, index):
    return jnp.take_along_axis(values, index, axis=1, mode="promise_in_bounds")


def kernel(
    n_tile, n_sec, step_ref, off_ref, frac_ref, mask_ref, out_ref,
    field, outer, edge, source, partial, turned, totals, base,
    index0, index1, col_frac, row_weight, flow_sum, degree,
    send_sem, recv_sem, total_send, total_recv,
):
    count = step_ref.shape[0]
    block = (count, LANES)
    f32 = jnp.float32
    tile = lax.axis_index("tile")
    sec = lax.axis_index("sec")
    span = UP + ROWS + DOWN
    halves = [slice(h * LANES, (h + 1) * LANES) for h in range(2)]

    def there(dt, ds):
        ok = None
        for here, d, n in ((tile, dt, n_tile), (sec, ds, n_sec)):
            if d:
                test = here + d < n if d > 0 else here + d >= 0
                ok = test if ok is None else jnp.logical_and(ok, test)
        return ok

    def clear(test, *places):
        @pl.when(test)
        def _():
            for ref in places:
                ref[...] = jnp.zeros(ref.shape, f32)

    clear(tile == 0, field.at[pl.ds(0, ITERS), pl.ds(0, UP)], edge.at[:, :, pl.ds(0, UP)])
    clear(tile == n_tile - 1, field.at[pl.ds(0, ITERS), pl.ds(UP + ROWS, DOWN)], edge.at[:, :, pl.ds(UP + ROWS, DOWN)])
    clear(sec == 0, edge.at[:, 0])
    clear(sec == n_sec - 1, edge.at[:, 1])

    barrier = pltpu.get_barrier_semaphore()

    def greet(peer):
        pl.semaphore_signal(barrier, inc=1, device_id=peer, device_id_type=MESH)

    for dt, ds in DIRECTIONS:
        if dt:

            @pl.when(there(dt, ds))
            def _():
                greet({"tile": tile + dt, "sec": sec + ds})

    for other in range(n_sec):

        @pl.when(sec != other)
        def _():
            greet({"sec": other})

    def beside(here, n):
        return jnp.where(here > 0, 1, 0) + jnp.where(here < n - 1, 1, 0)

    for c in range(2):
        for h in range(2):
            running = step_ref[0, c, :, halves[h]]
            turned[2 * c + h, 0] = running
            for s in range(1, count):
                running = running + step_ref[s, c, :, halves[h]]
                turned[2 * c + h, s] = running
            base[2 * c + h] = running

    pl.semaphore_wait(barrier, n_sec - 1 + beside(tile, n_tile) * (1 + beside(sec, n_sec)))

    def total_copy(origin, target):
        return pltpu.make_async_remote_copy(
            src_ref=base, dst_ref=totals.at[origin], send_sem=total_send.at[target],
            recv_sem=total_recv.at[origin], device_id={"sec": target}, device_id_type=MESH,
        )

    for origin in range(n_sec - 1):

        @pl.when(sec == origin)
        def _():
            for target in range(origin + 1, n_sec):
                total_copy(origin, target).start()

    for side in range(2):
        for h in range(2):
            for n, ref in enumerate((off_ref, frac_ref)):
                for c in range(2):
                    item = 8 * n + 4 * side + 2 * c + h
                    flipped = jnp.swapaxes(ref[:, side, c, :, halves[h]].astype(f32), 0, 1)
                    turned[4 + item] = flipped
            turned[20 + 2 * side + h] = jnp.swapaxes(mask_ref[:, side, :, halves[h]].astype(f32), 0, 1)

    lane = lax.broadcasted_iota(jnp.int32, block, 1)
    sub = lax.broadcasted_iota(jnp.int32, block, 0)
    section = sub + sec * count
    last_row = n_tile * ROWS - 1
    last_col = 2 * LANES - 1

    def prepare(r, carry):
        row = r + tile * ROWS
        flows = [[jnp.zeros(block, f32) for _ in range(2)] for _ in range(2)]
        live_count = []
        for h in range(2):
            column = lane + h * LANES
            four = jnp.where(row + 0 * column >= 1, 1.0, 0.0) + jnp.where(row + 0 * column <= last_row - 1, 1.0, 0.0)
            four = four + jnp.where(column >= 1, 1.0, 0.0) + jnp.where(column <= last_col - 1, 1.0, 0.0)
            live_count.append(four)
        for side in range(2):
            section_live = section >= 1 if side == 0 else section <= n_sec * count - 2
            parts = []
            for h in range(2):
                ro, co = (turned[4 + 4 * side + 2 * c + h, r].astype(jnp.int32) for c in range(2))
                rf, cf = (turned[12 + 4 * side + 2 * c + h, r] for c in range(2))
                target_row, target_col = row + ro, lane + h * LANES + co
                live = (target_row >= 0) & (target_row <= last_row - 1)
                live = live & (target_col >= 0) & (target_col <= last_col - 1)
                live = live & (turned[20 + 2 * side + h, r] == 1.0) & section_live
                live = jnp.where(live, 1.0, 0.0)
                flows[0][h] = flows[0][h] + live * (ro.astype(f32) + rf)
                flows[1][h] = flows[1][h] + live * (co.astype(f32) + cf)
                live_count[h] = live_count[h] + live
                parts.append((ro, co, live * (1.0 - rf), live * rf, cf))
            a, b = parts
            parts.append(tuple(middle_of(x, y, x, y) for x, y in zip(a, b)))
            for t, (ro, co, low, high, cf) in enumerate(parts):
                index0[r, side, t] = jnp.clip(lane + co, 0, LANES - 1)
                index1[r, side, t] = jnp.clip(lane + co + 1, 0, LANES - 1)
                col_frac[r, side, t] = cf
                for d in range(SHIFTS):
                    shift = d - REACH
                    row_weight[r, side, t, d] = jnp.where(ro == shift, low, jnp.where(ro == shift - 1, high, 0.0))
        for h in range(2):
            degree[r, h] = live_count[h]
            for c in range(2):
                flow_sum[r, 2 * c + h] = flows[c][h]
        return carry

    lax.fori_loop(0, ROWS, prepare, 0)

    for origin in range(n_sec - 1):

        @pl.when(sec > origin)
        def _():
            total_copy(origin, origin + 1).wait_recv()

        @pl.when(sec == origin)
        def _():
            for target in range(origin + 1, n_sec):
                total_copy(origin, target).wait_send()

    base[...] = jnp.zeros(base.shape, f32)
    for origin in range(n_sec - 1):

        @pl.when(sec > origin)
        def _():
            base[...] = base[...] + totals[origin]

    for k in range(4):
        field[0, UP:UP + ROWS, k] = jnp.swapaxes(turned[k] + base[k][None], 0, 1)

    sent_rows = {1: pl.ds(UP + ROWS - UP, UP), 0: pl.ds(UP, ROWS), -1: pl.ds(UP, DOWN)}
    landing_rows = {1: pl.ds(0, UP), 0: pl.ds(UP, ROWS), -1: pl.ds(UP + ROWS, DOWN)}

    def halo_copy(sweep, number):
        dt, ds = DIRECTIONS[number]
        if ds == 0:
            src, dst = field.at[sweep, sent_rows[dt]], field.at[sweep, landing_rows[dt]]
        else:
            which = 0 if ds > 0 else 1
            src, dst = outer.at[sweep, which, sent_rows[dt]], edge.at[sweep, which, landing_rows[dt]]
        peer = {}
        if dt:
            peer["tile"] = tile + dt
        if ds:
            peer["sec"] = sec + ds
        return pltpu.make_async_remote_copy(
            src_ref=src, dst_ref=dst,
            send_sem=send_sem.at[sweep, number], recv_sem=recv_sem.at[sweep, number],
            device_id=peer, device_id_type=MESH,
        )

    def arrive(sweep, diagonal_or_tile):
        for number, (dt, ds) in enumerate(DIRECTIONS):
            if (dt != 0) == diagonal_or_tile:

                @pl.when(there(-dt, -ds))
                def _():
                    halo_copy(sweep, number).wait_recv()

    def make_sources(sweep, rows):
        for q in rows:
            below, above = [], []
            for k in range(4):
                own = field[sweep, q, k]
                under = jnp.broadcast_to(edge[sweep, 0, q, k:k + 1, :], block)
                over = jnp.broadcast_to(edge[sweep, 1, q, k:k + 1, :], block)
                below.append(jnp.where(sub == 0, under, pltpu.roll(own, 1, 0)))
                above.append(jnp.where(sub == count - 1, over, pltpu.roll(own, count - 1, 0)))
            for side, parts in enumerate((below, above)):
                parts.append(middle_of(*parts))
                for k in range(5):
                    source[side, q, k] = parts[k]

    def gather_rows(r, wanted, sums):
        for side in range(2):
            i0 = [index0[r, side, t] for t in range(3)]
            i1 = [index1[r, side, t] for t in range(3)]
            cf = [col_frac[r, side, t] for t in range(3)]
            for d in range(SHIFTS):
                if not wanted(r + d):
                    continue
                weight = [row_weight[r, side, t, d] for t in range(3)]
                for k in range(5):
                    t = 2 if k == 4 else k % 2
                    values = source[side, r + d, k]
                    low, high = pick(values, i0[t]), pick(values, i1[t])
                    term = weight[t] * (low + cf[t] * (high - low))
                    sums[k] = term if sums[k] is None else sums[k] + term
        return sums

    def is_own(q):
        return UP <= q < UP + ROWS

    def relax(sweep, carry):
        for q in range(UP, UP + ROWS):
            for k in range(4):
                outer[sweep, 0, q, k:k + 1, :] = field[sweep, q, k, count - 1:count, :]
                outer[sweep, 1, q, k:k + 1, :] = field[sweep, q, k, 0:1, :]
        for number, (dt, ds) in enumerate(DIRECTIONS):

            @pl.when(there(dt, ds))
            def _():
                halo_copy(sweep, number).start()

        arrive(sweep, False)
        make_sources(sweep, range(UP, UP + ROWS))
        for r in range(ROWS):
            sums = gather_rows(r, is_own, [None] * 5)
            for k in range(5):
                partial[r, k] = sums[k]
        arrive(sweep, True)
        make_sources(sweep, [q for q in range(span) if not is_own(q)])
        for r in range(ROWS):
            sums = gather_rows(r, lambda q: not is_own(q), [partial[r, k] for k in range(5)])
            for c in range(2):
                seam = pltpu.roll(sums[4], 96 if c == 0 else 32, 1)
                cross = (
                    jnp.where(lane < 112, sums[2 * c], seam),
                    jnp.where(lane < 16, seam, sums[2 * c + 1]),
                )
                own = [field[sweep, UP + r, 2 * c + h] for h in range(2)]
                left = [pltpu.roll(x, 1, 1) for x in own]
                right = [pltpu.roll(x, LANES - 1, 1) for x in own]
                sides = (
                    jnp.where(lane == 0, 0.0, left[0]) + jnp.where(lane == LANES - 1, right[1], right[0]),
                    jnp.where(lane == 0, left[0], left[1]) + jnp.where(lane == LANES - 1, 0.0, right[1]),
                )
                for h in range(2):
                    k = 2 * c + h
                    above, below = field[sweep, UP + r - 1, k], field[sweep, UP + r + 1, k]
                    force = cross[h] + flow_sum[r, k] + sides[h] + (above + below) - degree[r, h] * own[h]
                    field[sweep + 1, UP + r, k] = own[h] + STEP * force
        for number, (dt, ds) in enumerate(DIRECTIONS):

            @pl.when(there(dt, ds))
            def _():
                halo_copy(sweep, number).wait_send()

        return carry

    lax.fori_loop(0, ITERS, relax, 0)
    for c in range(2):
        for h in range(2):
            out_ref[:, c, :, halves[h]] = jnp.swapaxes(field[ITERS, UP:UP + ROWS, 2 * c + h], 0, 1)


def per_device(n_tile, n_sec, step_field, offsets, fraction, flow_mask):
    count = step_field.shape[0]
    span = UP + ROWS + DOWN
    vmem = pl.BlockSpec(memory_space=pltpu.VMEM)
    f32, i32 = jnp.float32, jnp.int32
    return pl.pallas_call(
        functools.partial(kernel, n_tile, n_sec),
        out_shape=jax.ShapeDtypeStruct(step_field.shape, f32),
        in_specs=[vmem] * 4,
        out_specs=vmem,
        scratch_shapes=[
            pltpu.VMEM((ITERS + 1, span, 4, count, LANES), f32),
            pltpu.VMEM((ITERS, 2, span, 4, LANES), f32),
            pltpu.VMEM((ITERS, 2, span, 4, LANES), f32),
            pltpu.VMEM((2, span, 5, count, LANES), f32),
            pltpu.VMEM((ROWS, 5, count, LANES), f32),
            pltpu.VMEM((24, count, ROWS, LANES), f32),
            pltpu.VMEM((n_sec, 4, ROWS, LANES), f32),
            pltpu.VMEM((4, ROWS, LANES), f32),
            pltpu.VMEM((ROWS, 2, 3, count, LANES), i32),
            pltpu.VMEM((ROWS, 2, 3, count, LANES), i32),
            pltpu.VMEM((ROWS, 2, 3, count, LANES), f32),
            pltpu.VMEM((ROWS, 2, 3, SHIFTS, count, LANES), f32),
            pltpu.VMEM((ROWS, 4, count, LANES), f32),
            pltpu.VMEM((ROWS, 2, count, LANES), f32),
            pltpu.SemaphoreType.DMA((ITERS, len(DIRECTIONS))),
            pltpu.SemaphoreType.DMA((ITERS, len(DIRECTIONS))),
            pltpu.SemaphoreType.DMA((n_sec,)),
            pltpu.SemaphoreType.DMA((n_sec,)),
        ],
        compiler_params=pltpu.CompilerParams(
            collective_id=0, has_side_effects=True, vmem_limit_bytes=32 * 1024 * 1024
        ),
    )(step_field, offsets, fraction, flow_mask)


def solution(mesh):
    spec = P(("win", "sec"), None, "tile", None)
    flow_spec = P(("win", "sec"), None, None, "tile", None)
    return jax.shard_map(
        functools.partial(per_device, mesh.shape["tile"], mesh.shape["sec"]),
        mesh=mesh,
        in_specs=(spec, flow_spec, flow_spec, spec),
        out_specs=spec,
        check_vma=False,
    )
```

time: 55.2 us -> 41.5 us (0.75)
  the two profiles are of different devices: /device:TPU:0 before, /device:TPU:1 now
where the time goes in v2:
time: 41.5 us; the launch traced here: 41.3 us
  Pallas kernels  36.9 us (89%)
  local copies, waits for them, and re-layouts  4.36 us (11%)
    pallas_call x1, Pallas kernels, per_device(): pl.pallas_call(functools.partial(kernel, n_tile, n_sec), out_shape=jax.Sh...  36.9 us
    unnamed x9, local copies, waits for them, and re-layouts  4.36 us

profile of v2, /device:TPU:1, one launch (start us, length us, event | category | flops | bytes accessed | tf_op | source)
XLA Modules:
  0.0 41.3 jit_solution(7240699697299951135)
XLA Ops:
  0.0 0.0 copy-start
  0.0 0.9 %copy-done = s32[8,2,2,8,256]{4,3,2,1,0:T(8,128)S(1)} copy-done((s32[8,2,2,8,256]{4,3,2,1,0:T(8,128)S(1)}, s32[8,2,2,8,256]{4,3,2,1,0:T(8,128)}, u32[]{:S(2)}) %copy-start) | copy-done | bytes 262168
  1.0 0.0 copy-start.1
  1.0 0.9 %copy-done.1 = f32[8,2,2,8,256]{4,3,2,1,0:T(8,128)S(1)} copy-done((f32[8,2,2,8,256]{4,3,2,1,0:T(8,128)S(1)}, f32[8,2,2,8,256]{4,3,2,1,0:T(8,128)}, u32[]{:S(2)}) %copy-start.1) | copy-done | bytes 262168
  1.9 0.0 copy-start.2
  1.9 0.9 %copy-done.2 = f32[8,2,8,256]{3,2,1,0:T(8,128)S(1)} copy-done((f32[8,2,8,256]{3,2,1,0:T(8,128)S(1)}, f32[8,2,8,256]{3,2,1,0:T(8,128)}, u32[]{:S(2)}) %copy-start.2) | copy-done | bytes 131096
  2.8 0.0 copy-start.3
  2.8 0.9 %copy-done.3 = s32[8,2,8,256]{3,2,1,0:T(8,128)S(1)} copy-done((s32[8,2,8,256]{3,2,1,0:T(8,128)S(1)}, s32[8,2,8,256]{3,2,1,0:T(8,128)}, u32[]{:S(2)}) %copy-start.3) | copy-done | bytes 131096
  3.7 36.9 %shard_map.46 = f32[8,2,8,256]{3,2,1,0:T(8,128)S(1)} custom-call(f32[8,2,8,256]{3,2,1,0:T(8,128)S(1)} %copy-done.2, s32[8,2,2,8,256]{4,3,2,1,0:T(8,128)S(1)} %copy-done, f32[8,2,2,8,256]{4,3,2,1,0:T(8,128)S(1)} %copy-done.1, s32[8,2,8,256]{3,2,1,0:T(8,128)S(1)} %copy-done.3), custom_call_target="tpu_custom_call" | custom-call | tf_op jit(solution)/shard_map/pallas_call | solution.py:309
  40.6 0.7 %copy.6 = f32[8,2,8,256]{3,2,1,0:T(8,128)} copy(f32[8,2,8,256]{3,2,1,0:T(8,128)S(1)} %shard_map.46) | data formatting | bytes 262144
Async XLA Ops:
  0.0 0.9 %copy-start = (s32[8,2,2,8,256]{4,3,2,1,0:T(8,128)S(1)}, s32[8,2,2,8,256]{4,3,2,1,0:T(8,128)}, u32[]{:S(2)}) copy-start(s32[8,2,2,8,256]{4,3,2,1,0:T(8,128)} %off_ref.1) | copy-start | bytes 786436
  1.0 0.9 %copy-start.1 = (f32[8,2,2,8,256]{4,3,2,1,0:T(8,128)S(1)}, f32[8,2,2,8,256]{4,3,2,1,0:T(8,128)}, u32[]{:S(2)}) copy-start(f32[8,2,2,8,256]{4,3,2,1,0:T(8,128)} %frac_ref.1) | copy-start | bytes 786436
  1.9 0.9 %copy-start.2 = (f32[8,2,8,256]{3,2,1,0:T(8,128)S(1)}, f32[8,2,8,256]{3,2,1,0:T(8,128)}, u32[]{:S(2)}) copy-start(f32[8,2,8,256]{3,2,1,0:T(8,128)} %step_ref.1) | copy-start | bytes 393220
  2.8 0.9 %copy-start.3 = (s32[8,2,8,256]{3,2,1,0:T(8,128)S(1)}, s32[8,2,8,256]{3,2,1,0:T(8,128)}, u32[]{:S(2)}) copy-start(s32[8,2,8,256]{3,2,1,0:T(8,128)} %mask_ref.1) | copy-start | bytes 393220

commit v3 on v2

--- a/solution.py
+++ b/solution.py
@@ -31,11 +31,19 @@
 
 
 def kernel(
-    n_tile, n_sec, step_ref, off_ref, frac_ref, mask_ref, out_ref,
-    field, outer, edge, source, partial, turned, totals, base,
+    n_tile, n_sec, step_hbm, off_hbm, frac_hbm, mask_hbm, out_ref,
+    step_ref, off_ref, frac_ref, mask_ref, load_sem, field, outer, edge, source, partial, turned, totals, base,
     index0, index1, col_frac, row_weight, flow_sum, degree,
     send_sem, recv_sem, total_send, total_recv,
 ):
+    loads = [
+        pltpu.make_async_copy(far, near, load_sem.at[i])
+        for i, (far, near) in enumerate(
+            ((step_hbm, step_ref), (off_hbm, off_ref), (frac_hbm, frac_ref), (mask_hbm, mask_ref))
+        )
+    ]
+    for load in loads:
+        load.start()
     count = step_ref.shape[0]
     block = (count, LANES)
     f32 = jnp.float32
@@ -84,6 +92,7 @@
     def beside(here, n):
         return jnp.where(here > 0, 1, 0) + jnp.where(here < n - 1, 1, 0)
 
+    loads[0].wait()
     for c in range(2):
         for h in range(2):
             running = step_ref[0, c, :, halves[h]]
@@ -108,6 +117,8 @@
             for target in range(origin + 1, n_sec):
                 total_copy(origin, target).start()
 
+    for load in loads[1:]:
+        load.wait()
     for side in range(2):
         for h in range(2):
             for n, ref in enumerate((off_ref, frac_ref)):
@@ -248,17 +259,19 @@
     def is_own(q):
         return UP <= q < UP + ROWS
 
-    def relax(sweep, carry):
-        for q in range(UP, UP + ROWS):
+    def send(sweep, rows, wanted):
+        for q in rows:
             for k in range(4):
                 outer[sweep, 0, q, k:k + 1, :] = field[sweep, q, k, count - 1:count, :]
                 outer[sweep, 1, q, k:k + 1, :] = field[sweep, q, k, 0:1, :]
         for number, (dt, ds) in enumerate(DIRECTIONS):
-
-            @pl.when(there(dt, ds))
-            def _():
-                halo_copy(sweep, number).start()
-
+            if wanted(dt):
+
+                @pl.when(there(dt, ds))
+                def _():
+                    halo_copy(sweep, number).start()
+
+    def relax(sweep, carry):
         arrive(sweep, False)
         make_sources(sweep, range(UP, UP + ROWS))
         for r in range(ROWS):
@@ -287,15 +300,27 @@
                     above, below = field[sweep, UP + r - 1, k], field[sweep, UP + r + 1, k]
                     force = cross[h] + flow_sum[r, k] + sides[h] + (above + below) - degree[r, h] * own[h]
                     field[sweep + 1, UP + r, k] = own[h] + STEP * force
+            if r == DOWN - 1:
+
+                @pl.when(sweep < ITERS - 1)
+                def _():
+                    send(sweep + 1, range(UP, UP + DOWN), lambda dt: dt < 0)
+
+        @pl.when(sweep < ITERS - 1)
+        def _():
+            send(sweep + 1, range(UP + DOWN, UP + ROWS), lambda dt: dt >= 0)
+
+        return carry
+
+    send(0, range(UP, UP + ROWS), lambda dt: True)
+    lax.fori_loop(0, ITERS, relax, 0)
+    for sweep in range(ITERS):
         for number, (dt, ds) in enumerate(DIRECTIONS):
 
             @pl.when(there(dt, ds))
             def _():
                 halo_copy(sweep, number).wait_send()
 
-        return carry
-
-    lax.fori_loop(0, ITERS, relax, 0)
     for c in range(2):
         for h in range(2):
             out_ref[:, c, :, halves[h]] = jnp.swapaxes(field[ITERS, UP:UP + ROWS, 2 * c + h], 0, 1)
@@ -309,9 +334,14 @@
     return pl.pallas_call(
         functools.partial(kernel, n_tile, n_sec),
         out_shape=jax.ShapeDtypeStruct(step_field.shape, f32),
-        in_specs=[vmem] * 4,
+        in_specs=[pl.BlockSpec(memory_space=pl.ANY)] * 4,
         out_specs=vmem,
         scratch_shapes=[
+            pltpu.VMEM(step_field.shape, f32),
+            pltpu.VMEM(offsets.shape, i32),
+            pltpu.VMEM(fraction.shape, f32),
+            pltpu.VMEM(flow_mask.shape, i32),
+            pltpu.SemaphoreType.DMA((4,)),
             pltpu.VMEM((ITERS + 1, span, 4, count, LANES), f32),
             pltpu.VMEM((ITERS, 2, span, 4, LANES), f32),
             pltpu.VMEM((ITERS, 2, span, 4, LANES), f32),
@@ -332,7 +362,7 @@
             pltpu.SemaphoreType.DMA((n_sec,)),
         ],
         compiler_params=pltpu.CompilerParams(
-            collective_id=0, has_side_effects=True, vmem_limit_bytes=32 * 1024 * 1024
+            collective_id=0, has_side_effects=True, vmem_limit_bytes=60 * 1024 * 1024
         ),
     )(step_field, offsets, fraction, flow_mask)
 

time: 41.5 us -> 39 us (0.940)
  local copies, waits for them, and re-layouts: 4.36 us -> 1.57 us
    unnamed x9 -> x1, local copies, waits for them, and re-layouts: 4.36 us -> 1.57 us
where the time goes in v3:
time: 39 us; the launch traced here: 38.6 us
  Pallas kernels  37 us (95%)
  local copies, waits for them, and re-layouts  1.57 us (4%)
    pallas_call x1, Pallas kernels, per_device(): pl.pallas_call(functools.partial(kernel, n_tile, n_sec), out_shape=jax.Sh...  37 us
    unnamed x1, local copies, waits for them, and re-layouts  1.57 us

profile of v3, /device:TPU:1, one launch (start us, length us, event | category | flops | bytes accessed | tf_op | source)
XLA Modules:
  0.0 38.6 jit_solution(12882693401593153382)
XLA Ops:
  0.0 37.0 %shard_map.46 = f32[8,2,8,256]{3,2,1,0:T(8,128)} custom-call(f32[8,2,8,256]{3,2,1,0:T(8,128)} %step_hbm.1, s32[8,2,2,8,256]{4,3,2,1,0:T(8,128)} %off_hbm.1, f32[8,2,2,8,256]{4,3,2,1,0:T(8,128)} %frac_hbm.1, s32[8,2,8,256]{3,2,1,0:T(8,128)} %mask_hbm.1), custom_call_target="tpu_custom_call" | custom-call | tf_op jit(solution)/shard_map/pallas_call | solution.py:334
  37.0 1.6 %copy.6 = f32[8,2,8,256]{3,2,1,0:T(8,128)} copy(f32[8,2,8,256]{3,2,1,0:T(8,128)} %shard_map.46) | data formatting | bytes 262144
